TPU v7x, 512 devices: a whole 4x4x16 slice. The times are simulated.
512 devices in a mesh: dp: 64 (over x, z), tensor: 8 (over y, core).
Axes of the slice: x: 4, y: 4, z: 16, core: 2. Of those that a mesh axis runs over, the one named last changes fastest.
Arguments:
- query_states: bfloat16 [256, 64, 4096], P('dp', None, 'tensor'), may hold values from -300 to 300
- passage_states: bfloat16 [256, 64, 4096], P('dp', None, 'tensor'), may hold values from -300 to 300
- negative_states: bfloat16 [256, 64, 4096], P('dp', None, 'tensor'), may hold values from -300 to 300
- query_len: int32 [256], P('dp'), may hold values from 4 to 64
- passage_len: int32 [256], P('dp'), may hold values from 4 to 64
- negative_len: int32 [256], P('dp'), may hold values from 4 to 64
- norm_gain: float32 [4096], P('tensor'), may hold values from 0.5 to 1.5
- proj_weight: bfloat16 [4096, 768], P('tensor'), may hold values from -0.09375 to 0.09375
- neg_owner: int32 [256, 7], P('dp'), may hold values from 0 to 63, all different within a row; in each aligned block of 4 rows (0 to 3, 4 to 7, ...) at most 4 rows name the same one
- neg_slot: int32 [256, 7], P('dp'), may hold values from 0 to 3
Outputs:
- grad_queries: bfloat16 [256, 64, 4096], P('dp', None, 'tensor')
- grad_passages: bfloat16 [256, 64, 4096], P('dp', None, 'tensor')
- grad_negatives: bfloat16 [256, 64, 4096], P('dp', None, 'tensor')
- grad_weight: bfloat16 [4096, 768], P('tensor')
- grad_gain: float32 [4096], P('tensor')
- loss: float32 [], replicated
Inputs may be any that keep to these rules, and one draw needn't show every extreme that they name: `neg_owner`: each query names 7 different owners; among the 4 queries of one dp index no owner is named more than 4 times, and one owner exactly 4 times.
All inputs are finite; a program needn't handle non-finite values.
Results may differ from a plain program's by a relative error of at most 0.0017.
Values sent between devices are 32-bit elements; how exact they have to be, the bound alone decides.
A program may use at most 64 MiB of HBM per device.

v0:
```python
import jax
import jax.numpy as jnp
from jax import lax
from jax.sharding import PartitionSpec as P

D = 4096


score_scale = 20.0
loss_scale = 1024.0
epsilon = 1e-06
highest = lax.Precision.HIGHEST


def body(
    query_states,
    passage_states,
    negative_states,
    query_len,
    passage_len,
    negative_len,
    norm_gain,
    proj_weight,
    neg_owner,
    neg_slot,
):
    pairs = query_states.shape[0]
    token_slots = query_states.shape[1]
    shards = lax.axis_size("dp")
    shard = lax.axis_index("dp")
    stacks = (query_states, passage_states, negative_states)
    weight = proj_weight.astype(jnp.float32)
    lengths = jnp.stack([query_len, passage_len, negative_len]).astype(jnp.float32)
    positions = jnp.arange(token_slots)
    live = jnp.where(positions[None, None, :] < lengths[:, :, None], 1.0 / lengths[:, :, None], 0.0)
    squares = jnp.stack([jnp.sum(jnp.square(s.astype(jnp.float32)), -1) for s in stacks])
    squares = lax.psum(squares, "tensor")
    scales = lax.rsqrt(squares / D + epsilon)
    coeffs = scales * live
    plain = jnp.concatenate(
        [jnp.sum(stacks[i].astype(jnp.float32) * coeffs[i][:, :, None], 1) for i in range(3)], 0
    )
    pooled = plain * norm_gain
    proj = lax.psum(jnp.dot(pooled, weight, precision=highest), "tensor")
    norms = jnp.sqrt(jnp.sum(proj * proj, -1, keepdims=True) + epsilon)
    unit = proj / norms
    uq = unit[:pairs]
    up = unit[pairs : 2 * pairs]
    un = unit[2 * pairs :]
    count_negs = neg_owner.shape[1]
    flat_ids = (neg_owner * pairs + neg_slot).reshape(-1)
    up_all, un_all = (
        lax.all_gather(up, "dp", axis=0, tiled=True),
        lax.all_gather(un, "dp", axis=0, tiled=True),
    )
    negrows = jnp.take(un_all, flat_ids, axis=0)
    all_pairs = up_all.shape[0]
    negs = negrows.reshape(pairs, count_negs, -1)
    s_in = score_scale * jnp.dot(uq, up_all.T, precision=highest)
    s_neg = score_scale * jnp.einsum("qe,qke->qk", uq, negs, precision=highest)
    ex_in = jnp.exp(s_in)
    ex_neg = jnp.exp(s_neg)
    total = jnp.sum(ex_in, 1) + jnp.sum(ex_neg, 1)
    logtotal = jnp.log(total)
    own_cols = shard * pairs + jnp.arange(pairs)
    target = (jnp.arange(all_pairs)[None, :] == own_cols[:, None]).astype(jnp.float32)
    loss_local = jnp.sum(logtotal - jnp.sum(s_in * target, 1))
    g_in = loss_scale * (ex_in / total[:, None] - target)
    g_neg = loss_scale * ex_neg / total[:, None]
    d_uq = score_scale * (
        jnp.dot(g_in, up_all, precision=highest)
        + jnp.einsum("qk,qke->qe", g_neg, negs, precision=highest)
    )
    terms = score_scale * jnp.dot(g_in.T, uq, precision=highest)
    d_up = lax.psum_scatter(terms, "dp", scatter_dimension=0, tiled=True)
    d_negrows = (score_scale * g_neg[:, :, None] * uq[:, None, :]).reshape(pairs * count_negs, -1)
    spread = (flat_ids[None, :] == jnp.arange(all_pairs)[:, None]).astype(jnp.float32)
    neg_terms = jnp.dot(spread, d_negrows, precision=highest)
    d_un = lax.psum_scatter(neg_terms, "dp", scatter_dimension=0, tiled=True)
    d_unit = jnp.concatenate([d_uq, d_up, d_un], 0)
    d_proj = (d_unit - unit * jnp.sum(unit * d_unit, -1, keepdims=True)) / norms
    weight_part = jnp.dot(pooled.T, d_proj, precision=highest)
    d_pooled = jnp.dot(d_proj, weight.T, precision=highest)
    gain_part = jnp.sum(d_pooled * plain, 0)
    lifted = (d_pooled * norm_gain).reshape(3, pairs, -1)
    dots = jnp.stack(
        [jnp.sum(stacks[i].astype(jnp.float32) * lifted[i][:, None, :], -1) for i in range(3)]
    )
    dots = lax.psum(dots, "tensor")
    grads = []
    for i in range(3):
        inner = scales[i] * scales[i] / D * dots[i]
        value = coeffs[i][:, :, None] * (
            lifted[i][:, None, :] - stacks[i].astype(jnp.float32) * inner[:, :, None]
        )
        grads.append(value.astype(jnp.bfloat16))
    weight_sum, gain_sum, loss_sum = lax.psum((weight_part, gain_part, loss_local), "dp")
    weight_scaled = weight_sum / loss_scale
    return (
        grads[0],
        grads[1],
        grads[2],
        weight_scaled.astype(jnp.bfloat16),
        gain_sum / loss_scale,
        loss_sum / (shards * pairs),
    )


def solution(mesh):
    placed = (
        P("dp", None, "tensor"),
        P("dp", None, "tensor"),
        P("dp", None, "tensor"),
        P("dp"),
        P("dp"),
        P("dp"),
        P("tensor"),
        P("tensor", None),
        P("dp", None),
        P("dp", None),
    )
    return jax.shard_map(
        body,
        mesh=mesh,
        in_specs=placed,
        out_specs=(
            P("dp", None, "tensor"),
            P("dp", None, "tensor"),
            P("dp", None, "tensor"),
            P("tensor", None),
            P("tensor"),
            P(),
        ),
        check_vma=False,
    )
```

profile of v0, /device:TPU:1, one launch (start us, length us, event | category | flops | bytes accessed | tf_op | source)
XLA Modules:
  0.0 816.3 jit_solution(3546986910048487336)
XLA Ops:
  7.2 0.8 add_convert_fusion
  8.0 0.7 broadcast_divide_fusion.1
  8.7 0.7 compare_and_fusion
  9.6 1.1 fusion.1
  10.7 1.1 fusion.7
  11.8 1.1 fusion.13
  12.9 18.9 %psum.42 = f32[3,4,64]{2,1,0:T(4,128)S(1)} all-reduce(f32[3,4,64]{2,1,0:T(4,128)S(1)} %pad_maximum_fusion.4), channel_id=1, replica_groups=mesh['dp'=64,'tensor'=8] {'tensor'}, use_global_device_ids=true, to_apply=%region_3.4 | all-reduce | flops 768 | bytes 6144 | tf_op jit(solution)/shard_map/psum | solution.py:37
  31.8 1.1 fusion.14
  32.9 1.2 fusion.2
  34.6 21.5 %psum.43 = f32[12,768]{1,0:T(8,128)S(1)} all-reduce(f32[12,768]{1,0:T(8,128)S(1)} %fusion.33), channel_id=1, replica_groups=mesh['dp'=64,'tensor'=8] {'tensor'}, use_global_device_ids=true, to_apply=%region_7.8 | all-reduce | flops 9216 | bytes 73728 | tf_op jit(solution)/shard_map/psum | solution.py:44
  56.3 78.0 %all-gather.1 = f32[64,4,768]{2,1,0:T(4,128)S(1)} all-gather(f32[1,4,768]{2,1,0:T(4,128)S(1)} %get-tuple-element.19), channel_id=1, replica_groups=mesh['dp'=64,'tensor'=8] {'dp'}, dimensions={0}, use_global_device_ids=true | all-gather | bytes 798720 | tf_op jit(solution)/shard_map/all_gather | solution.py:54
  134.6 0.6 gather_fusion
  135.7 73.5 %all-gather = f32[64,4,768]{2,1,0:T(4,128)S(1)} all-gather(f32[1,4,768]{2,1,0:T(4,128)S(1)} %get-tuple-element.20), channel_id=1, replica_groups=mesh['dp'=64,'tensor'=8] {'dp'}, dimensions={0}, use_global_device_ids=true | all-gather | bytes 798720 | tf_op jit(solution)/shard_map/all_gather | solution.py:53
  209.5 0.8 select_reduce_fusion
  210.4 0.6 subtract_reduce_fusion
  211.0 1.8 convolution_multiply_fusion
  213.0 1.4 fusion.19
  214.5 1.3 dynamic-slice
  216.7 0.5 fusion
  217.1 312.0 %all-reduce.9.cloned.1.call-done = (f32[256,768]{1,0:T(8,128)}, f32[256,768]{1,0:T(8,128)}) async-done(((f32[256,768]{1,0:T(8,128)}, f32[256,768]{1,0:T(8,128)}), (f32[256,768]{1,0:T(8,128)}, f32[256,768]{1,0:T(8,128)})) %all-reduce.9.cloned.1.call-update) | async-done | bytes 1572880
  529.2 0.7 constant_dynamic-slice_fusion
  529.9 0.7 constant_dynamic-slice_fusion.1
  530.8 0.8 multiply_reduce_fusion.2
  531.6 2.6 fusion.31
  534.4 113.0 %all-reduce.2 = (f32[512]{0:T(512)S(1)}, f32[]{:T(128)}) all-reduce(f32[512]{0:T(512)S(1)} %get-tuple-element.22, f32[]{:T(128)} %get-tuple-element.12), channel_id=1, replica_groups=mesh['dp'=64,'tensor'=8] {'dp'}, use_global_device_ids=true, to_apply=%region_20.21 | all-reduce | flops 513 | bytes 4104 | tf_op jit(solution)/shard_map/psum | solution.py:97
  648.3 49.9 %psum.44 = f32[3,4,64]{2,1,0:T(4,128)S(1)} all-reduce(f32[3,4,64]{2,1,0:T(4,128)S(1)} %pad_maximum_fusion.5), channel_id=1, replica_groups=mesh['dp'=64,'tensor'=8] {'tensor'}, use_global_device_ids=true, to_apply=%region_17.18 | all-reduce | flops 768 | bytes 6144 | tf_op jit(solution)/shard_map/psum | solution.py:89
  698.2 0.6 broadcast_multiply_fusion.1
  698.8 0.9 fusion.18
  699.7 0.9 fusion.12
  700.5 0.9 fusion.6
  701.4 104.6 %all-reduce.7.cloned.1.call-done = f32[512,768]{1,0:T(8,128)} async-done(((f32[512,768]{1,0:T(8,128)}), f32[512,768]{1,0:T(8,128)}) %all-reduce.7.cloned.1.call-update) | async-done | bytes 1572880 | tf_op jit(solution)/shard_map/psum | solution.py:97
  806.0 2.4 multiply_convert_fusion
  (45 shorter events, 3.2 us)
Async XLA Ops:
  7.2 27.0 %copy-start = (bf16[512,768]{1,0:T(8,128)(2,1)S(1)}, bf16[512,768]{1,0:T(8,128)(2,1)}, u32[]{:S(2)}) copy-start(bf16[512,768]{1,0:T(8,128)(2,1)} %param.17) | copy-start | bytes 2359300
  7.2 27.0 %copy-start.4 = (f32[512]{0:T(512)S(1)}, f32[512]{0:T(512)}, u32[]{:S(2)}) copy-start(f32[512]{0:T(512)} %param.16) | copy-start | bytes 6148
  7.2 522.0 %all-reduce.9.cloned.1.call-start = ((), (), s32[]{:S(2)}) async-start(), calls=%async_computation.1 | async-start | bytes 3145728
  214.4 591.6 %all-reduce.7.cloned.1.call-start = ((), (), s32[]{:S(2)}) async-start(), calls=%async_computation | async-start | bytes 3145728 | tf_op jit(solution)/shard_map/psum | solution.py:97
  531.6 2.7 copy-start.3
  531.6 116.4 %copy-start.2 = (bf16[4,64,512]{2,1,0:T(8,128)(2,1)S(1)}, bf16[4,64,512]{2,1,0:T(8,128)(2,1)}, u32[]{:S(2)}) copy-start(bf16[4,64,512]{2,1,0:T(8,128)(2,1)} %param.11) | copy-start | bytes 786436
  531.6 116.6 %copy-start.1 = (bf16[4,64,512]{2,1,0:T(8,128)(2,1)S(1)}, bf16[4,64,512]{2,1,0:T(8,128)(2,1)}, u32[]{:S(2)}) copy-start(bf16[4,64,512]{2,1,0:T(8,128)(2,1)} %param.12) | copy-start | bytes 786436
Sparse Core Ops, SparseCore 0:
  214.5 314.5 all-reduce.8
  534.4 271.5 all-reduce.6
where the time goes:
time: 825 us; the launch traced here: 816 us
  waiting for transfers between devices  417 us (51%)
  blocking collectives  355 us (43%)
  between operations  16.7 us (2%)
  other arithmetic  15 us (2%)
  matrix products  8.97 us (1%)
    unnamed x3, waiting for transfers between devices  312 us
    psum x1, blocking collectives, body(): lax.psum((weight_part, gain_part, loss_local), 'dp')  113 us
    psum x1, waiting for transfers between devices, body(): lax.psum((weight_part, gain_part, loss_local), 'dp')  105 us
    all_gather x1, blocking collectives, body(): lax.all_gather(un, 'dp', axis=0, tiled=True)  78 us
    all_gather x1, blocking collectives, body(): lax.all_gather(up, 'dp', axis=0, tiled=True)  73.5 us
    psum x1, blocking collectives, body(): dots = lax.psum(dots, 'tensor')  49.9 us
    psum x1, blocking collectives, body(): proj = lax.psum(jnp.dot(pooled, weight, precision=highest), 'tensor')  21.5 us
    psum x1, blocking collectives, body(): squares = lax.psum(squares, 'tensor')  18.9 us
  transfers between devices with their start and end apart: 2, of which 2 were waited for; matrix products, arithmetic and copies ran while one was open for 1% of the time, Pallas kernels for 0%

commit v1 on v0

v1 whole, which is shorter than its diff:
```python
import jax
import jax.numpy as jnp
from jax import lax
from jax.experimental import pallas as pl
from jax.experimental.pallas import tpu as pltpu
from jax.sharding import PartitionSpec as P

NX, NY, NZ, NC = 4, 4, 16, 2
NT = NY * NC
DP = NX * NZ
D = 4096
F = D // NT
E = 768
H = E // NC
LEN = 64
SLOTS = 4
NEGS = 7
KINDS = 3
TOK = KINDS * SLOTS * LEN
ALL = SLOTS * DP
SEQ = KINDS * ALL
score_scale = 20.0
loss_scale = 1024.0
epsilon = 1e-06
MESH = pl.DeviceIdType.MESH
f32 = jnp.float32
bf16 = jnp.bfloat16
NN = (((1,), (0,)), ((), ()))
NTD = (((1,), (1,)), ((), ()))


def dot(a, b, dims=NN):
    return lax.dot_general(a, b, dims, preferred_element_type=f32)


def exact_dot(a, b, dims=NN):
    return lax.dot_general(a, b, dims, preferred_element_type=f32, precision=lax.Precision.HIGHEST)


def split2(v):
    hi = v.astype(bf16)
    return hi, (v - hi.astype(f32)).astype(bf16)


def split3(v):
    hi = v.astype(bf16)
    rest = v - hi.astype(f32)
    mid = rest.astype(bf16)
    return jnp.concatenate([hi, mid, (rest - mid.astype(f32)).astype(bf16)], 0)


def join3(v):
    return v[0:16] + v[16:32] + v[32:48]


def dot3(a, b, dims=NN):
    return dot(a[0], b[0], dims) + (dot(a[0], b[1], dims) + dot(a[1], b[0], dims))


def kernel(
    x_refs,
    len_refs,
    gain_ref,
    w_ref,
    owner_ref,
    slot_ref,
    g_refs,
    gw_ref,
    gg_ref,
    loss_ref,
    xs,
    sq_own,
    sq_land,
    dot_own,
    dot_land,
    stage,
    rs_land,
    ids_ref,
    L,
    PB,
    u_hi,
    u_lo,
    dproj,
    own_rows,
    s_sq,
    r_sq,
    s_rs,
    r_rs,
    s_z,
    r_z,
    s_a,
    r_a,
    s_b,
    r_b,
    s_c,
    r_c,
    s_dot,
    r_dot,
    s_px,
    r_px,
    s_pz,
    r_pz,
):
    dp = lax.axis_index("dp")
    t = lax.axis_index("tensor")
    x, z = dp // NZ, dp % NZ
    y, c = t // NC, t % NC
    a = jnp.where(c == 0, x, y)
    b = jnp.where(c == 0, y, x)

    def tensor_peer(k):
        return (dp, (t + k) % NT)

    def x_peer(k):
        return (((x + k) % NX) * NZ + z, t)

    def y_peer(k):
        return (dp, ((y + k) % NY) * NC + c)

    def z_peer(k):
        return (x * NZ + (z + k) % NZ, t)

    def either(cond, p, q):
        return tuple(jnp.where(cond, i, j) for i, j in zip(p, q))

    def a_peer(k):
        return either(c == 0, x_peer(k), y_peer(k))

    def b_peer(k):
        return either(c == 0, y_peer(k), x_peer(k))

    sibling = (dp, y * NC + 1 - c)

    def send(src, dst, ss, rs, to):
        cp = pltpu.make_async_remote_copy(
            src_ref=src, dst_ref=dst, send_sem=ss, recv_sem=rs, device_id=to, device_id_type=MESH
        )
        cp.start()
        return cp

    barrier = pltpu.get_barrier_semaphore()
    greeted = (
        [tensor_peer(k) for k in range(1, NT)]
        + [x_peer(k) for k in range(1, NX)]
        + [z_peer(k) for k in range(1, NZ)]
    )
    for peer in greeted:
        pl.semaphore_signal(barrier, inc=1, device_id=peer, device_id_type=MESH)

    for i in range(KINDS):
        xs[pl.ds(i * SLOTS * LEN, SLOTS * LEN), :] = x_refs[i][...]
    xf = xs[...].astype(f32)
    xf = xf * xf
    part = (xf[:, 0:128] + xf[:, 128:256]) + (xf[:, 256:384] + xf[:, 384:512])
    sq_own[...] = exact_dot(jnp.ones((8, 128), f32), part, NTD)[0:1]

    pl.semaphore_wait(barrier, len(greeted))

    def tensor_sum(own, land, ss, rs):
        cps = [send(own, land.at[t], ss.at[k - 1], rs.at[k - 1], tensor_peer(k)) for k in range(1, NT)]
        land[t] = own[...]
        for cp in cps:
            cp.wait()
        total = land[0]
        for i in range(1, NT):
            total = total + land[i]
        return total

    squares = tensor_sum(sq_own, sq_land, s_sq, r_sq)
    scales = lax.rsqrt(squares / D + epsilon)
    lane = lax.broadcasted_iota(jnp.int32, (1, TOK), 1)
    seq = lane // LEN
    lens = jnp.zeros((1, TOK), jnp.int32)
    for i in range(KINDS):
        for s in range(SLOTS):
            lens = jnp.where(seq == i * SLOTS + s, len_refs[i][s], lens)
    live = jnp.where(lane % LEN < lens, 1.0 / lens.astype(f32), 0.0)
    coeffs = scales * live
    row = lax.broadcasted_iota(jnp.int32, (16, TOK), 0)
    mine = (row % 4) * SLOTS + row // 4 == seq
    plain = join3(dot(split3(jnp.where(mine, coeffs, 0.0)), xs[...]))
    PB[x, z] = plain
    px = [
        send(PB.at[x, z], PB.at[x, z], s_px.at[k - 1], r_px.at[k - 1], x_peer(k))
        for k in range(1, NX)
    ]
    gain = gain_ref[...]
    proj = join3(dot(split3(plain * gain), w_ref[...]))
    for s in range(SLOTS):
        for h in range(NC):
            stage[s * NC + h] = proj[4 * s : 4 * s + 4, h * H : (h + 1) * H]
    cps = [
        send(stage.at[(t + k) % NT], rs_land.at[t], s_rs.at[k - 1], r_rs.at[k - 1], tensor_peer(k))
        for k in range(1, NT)
    ]
    rs_land[t] = stage[t]
    ids = (slot_ref[...] * DP + owner_ref[...]).astype(f32)
    ids_ref[...] = jnp.zeros_like(ids_ref)
    for s in range(SLOTS):
        ids_ref[s, :, 0:NEGS] = ids[s : s + 1]
    for cp in cps:
        cp.wait()
    piece = rs_land[0]
    for i in range(1, NT):
        piece = piece + rs_land[i]
    place = lax.broadcasted_iota(jnp.int32, (4, H), 0)
    at = (b * 4 + a) * NZ + z
    L[c, at] = jnp.where(place == 3, ids_ref[y], piece)

    zs = [send(L.at[c, at], L.at[c, at], s_z.at[k - 1], r_z.at[k - 1], z_peer(k)) for k in range(1, NZ)]

    for cp in px:
        cp.wait()

    def ring(step):
        out = []
        if step <= 8:
            up = PB.at[:, (z - step + 1 + NZ) % NZ]
            out.append(send(up, up, s_pz.at[0, step - 1], r_pz.at[0, step - 1], z_peer(1)))
        if step <= 7:
            down = PB.at[:, (z + step - 1) % NZ]
            out.append(send(down, down, s_pz.at[1, step - 1], r_pz.at[1, step - 1], z_peer(NZ - 1)))
        return out

    turn = ring(1)

    def next_turn(turn, step):
        for cp in turn:
            cp.wait()
        return ring(step)

    for cp in zs:
        cp.wait()
    line = L.at[c, pl.ds((b * 4 + a) * NZ, NZ)]
    cps = [send(line, line, s_a.at[k - 1], r_a.at[k - 1], a_peer(k)) for k in range(1, 4)]
    turn = next_turn(turn, 2)
    for cp in cps:
        cp.wait()
    plane = L.at[c, pl.ds(b * 64, 64)]
    cps = [send(plane, plane, s_b.at[k - 1], r_b.at[k - 1], b_peer(k)) for k in range(1, 4)]
    across = [send(plane, plane, s_c.at[0], r_c.at[0], sibling)]
    turn = next_turn(turn, 3)
    for k in (1, 3, 2):
        cps[k - 1].wait()
        got = L.at[c, pl.ds(((b + 4 - k) % 4) * 64, 64)]
        across.append(send(got, got, s_c.at[k], r_c.at[k], sibling))
        turn = next_turn(turn, {1: 4, 3: 5, 2: 6}[k])
    for cp in across:
        cp.wait()

    for k in range(KINDS):
        for s in range(SLOTS):
            left = L[0, pl.ds(s * 64, 64), k, :]
            right = jnp.concatenate(
                [L[1, pl.ds(i * 64 + s * NZ, NZ), k, :] for i in range(NX)], 0
            )
            dproj[pl.ds(k * ALL + s * DP, DP), pl.ds(0, H)] = left
            dproj[pl.ds(k * ALL + s * DP, DP), pl.ds(H, H)] = right
    projs = dproj[...]
    r_norm = lax.rsqrt(jnp.sum(projs * projs, -1, keepdims=True) + epsilon)
    unit = projs * r_norm
    hi, lo = split2(unit)
    u_hi[...] = hi
    u_lo[...] = lo
    turn = next_turn(turn, 7)

    def part_of(k):
        rows = pl.ds(k * ALL, ALL)
        return u_hi[rows, :], u_lo[rows, :]

    uq, up, un = part_of(0), part_of(1), part_of(2)
    s_in = score_scale * dot3(uq, up, NTD)
    s_neg = score_scale * dot3(uq, un, NTD)
    lanes = lax.broadcasted_iota(jnp.int32, (ALL, ALL), 1)
    diag = lax.broadcasted_iota(jnp.int32, (ALL, ALL), 0) == lanes
    all_ids = L[0, :, 3, 0:128].astype(jnp.int32)
    named = lanes == all_ids[:, 0:1]
    for k in range(1, NEGS):
        named = jnp.logical_or(named, lanes == all_ids[:, k : k + 1])
    ex_in = jnp.exp(s_in)
    ex_neg = jnp.where(named, jnp.exp(s_neg), 0.0)
    total = jnp.sum(ex_in, 1, keepdims=True) + jnp.sum(ex_neg, 1, keepdims=True)
    own_score = jnp.sum(jnp.where(diag, s_in, 0.0), 1, keepdims=True)
    loss_ref[...] = jnp.sum(jnp.log(total) - own_score, 0, keepdims=True) / ALL
    factor = (score_scale * loss_scale) / total
    g_in = ex_in * factor - jnp.where(diag, score_scale * loss_scale, 0.0)
    g_neg = ex_neg * factor
    turn = next_turn(turn, 8)
    d_uq = dot3(split2(g_in), up) + dot3(split2(g_neg), un)
    d_up = dot3(split2(g_in.T), uq)
    d_un = dot3(split2(g_neg.T), uq)
    d_unit = jnp.concatenate([d_uq, d_up, d_un], 0)
    dproj[...] = (d_unit - unit * jnp.sum(unit * d_unit, -1, keepdims=True)) * r_norm

    own_rows[...] = jnp.zeros_like(own_rows)
    for s in range(SLOTS):
        for k in range(KINDS):
            own_rows[4 * s + k : 4 * s + k + 1, :] = dproj[pl.ds(k * ALL + s * DP + dp, 1), :]
    d_pooled = join3(dot(split3(own_rows[...]), w_ref[...], NTD))
    lifted = d_pooled * gain
    spread = join3(dot(split3(lifted), xs[...], NTD))
    dot_own[...] = jnp.sum(jnp.where(mine, spread, 0.0), 0, keepdims=True)
    for cp in turn:
        cp.wait()
    dots = tensor_sum(dot_own, dot_land, s_dot, r_dot)

    inner = scales * scales / D * dots
    rows = jnp.concatenate([coeffs, coeffs * inner, jnp.zeros((6, TOK), f32)], 0)
    cols = rows.T
    for i in range(KINDS):
        for s in range(SLOTS):
            at = (i * SLOTS + s) * LEN
            value = cols[at : at + LEN, 0:1] * lifted[4 * s + i : 4 * s + i + 1, :] - (
                xs[pl.ds(at, LEN), :].astype(f32) * cols[at : at + LEN, 1:2]
            )
            g_refs[i][pl.ds(s * LEN, LEN), :] = value.astype(bf16)

    plain_all = jnp.concatenate(
        [
            jnp.concatenate([PB[i, :, 4 * s + k, :] for i in range(NX)], 0)
            for k in range(KINDS)
            for s in range(SLOTS)
        ],
        0,
    )
    grad = dot3(split2(plain_all.T), split2(dproj[...])) / loss_scale
    gg_ref[...] = exact_dot(jnp.ones((8, E), f32), grad * w_ref[...].astype(f32), NTD)[0:1]
    gw_ref[...] = (grad * gain.T).astype(bf16)


def body(q, p, n, q_len, p_len, n_len, gain, w, owner, slot):
    vmem = pl.BlockSpec(memory_space=pltpu.VMEM)
    smem = pl.BlockSpec(memory_space=pltpu.SMEM)
    dma = pltpu.SemaphoreType.DMA
    states = [v.reshape(SLOTS * LEN, F) for v in (q, p, n)]

    def run(x0, x1, x2, l0, l1, l2, gain_ref, w_ref, owner_ref, slot_ref, g0, g1, g2, *rest):
        kernel((x0, x1, x2), (l0, l1, l2), gain_ref, w_ref, owner_ref, slot_ref, (g0, g1, g2), *rest)

    state_out = jax.ShapeDtypeStruct((SLOTS * LEN, F), bf16)
    g0, g1, g2, gw, gg, loss = pl.pallas_call(
        run,
        out_shape=(
            state_out,
            state_out,
            state_out,
            jax.ShapeDtypeStruct((F, E), bf16),
            jax.ShapeDtypeStruct((1, F), f32),
            jax.ShapeDtypeStruct((1, 1), f32),
        ),
        in_specs=[vmem] * 3 + [smem] * 3 + [vmem] * 4,
        out_specs=(vmem,) * 6,
        scratch_shapes=[
            pltpu.VMEM((TOK, F), bf16),
            pltpu.VMEM((1, TOK), f32),
            pltpu.VMEM((NT, 1, TOK), f32),
            pltpu.VMEM((1, TOK), f32),
            pltpu.VMEM((NT, 1, TOK), f32),
            pltpu.VMEM((NT, 4, H), f32),
            pltpu.VMEM((NT, 4, H), f32),
            pltpu.VMEM((SLOTS, 1, H), f32),
            pltpu.VMEM((NC, ALL, 4, H), f32),
            pltpu.VMEM((NX, NZ, 16, F), f32),
            pltpu.VMEM((SEQ, E), bf16),
            pltpu.VMEM((SEQ, E), bf16),
            pltpu.VMEM((SEQ, E), f32),
            pltpu.VMEM((16, E), f32),
            dma((NT - 1,)),
            dma((NT - 1,)),
            dma((NT - 1,)),
            dma((NT - 1,)),
            dma((NZ - 1,)),
            dma((NZ - 1,)),
            dma((3,)),
            dma((3,)),
            dma((3,)),
            dma((3,)),
            dma((4,)),
            dma((4,)),
            dma((NT - 1,)),
            dma((NT - 1,)),
            dma((3,)),
            dma((3,)),
            dma((2, 8)),
            dma((2, 8)),
        ],
        compiler_params=pltpu.CompilerParams(
            collective_id=0, has_side_effects=True, vmem_limit_bytes=50 << 20
        ),
    )(*states, q_len, p_len, n_len, gain.reshape(1, F), w, owner, slot)
    shape = q.shape
    return (
        g0.reshape(shape),
        g1.reshape(shape),
        g2.reshape(shape),
        gw,
        gg.reshape(F),
        loss.reshape(()),
    )


def solution(mesh):
    placed = (
        P("dp", None, "tensor"),
        P("dp", None, "tensor"),
        P("dp", None, "tensor"),
        P("dp"),
        P("dp"),
        P("dp"),
        P("tensor"),
        P("tensor", None),
        P("dp", None),
        P("dp", None),
    )
    return jax.shard_map(
        body,
        mesh=mesh,
        in_specs=placed,
        out_specs=(
            P("dp", None, "tensor"),
            P("dp", None, "tensor"),
            P("dp", None, "tensor"),
            P("tensor", None),
            P("tensor"),
            P(),
        ),
        check_vma=False,
    )
```

time: 825 us -> 94 us (0.11)
  waiting for transfers between devices: 417 us -> 0 us
  blocking collectives: 355 us -> 0 us
  Pallas kernels: 0 us -> 82.5 us
  other arithmetic: 15 us -> 0 us
  between operations: 16.7 us -> 2.46 us
  matrix products: 8.97 us -> 0 us
    unnamed x3 -> x0, waiting for transfers between devices: 312 us -> none
    psum x4 -> x0, blocking collectives: 203 us -> none  [the longest x1 113 us: body(): lax.psum((weight_part, gain_part, loss_local), 'dp')]
    all_gather x2 -> x0, blocking collectives: 152 us -> none  [the longest x1 78 us: body(): lax.all_gather(un, 'dp', axis=0, tiled=True)]
    psum x1 -> x0, waiting for transfers between devices: 105 us -> none  [body(): lax.psum((weight_part, gain_part, loss_local), 'dp')]
    pallas_call x0 -> x1, Pallas kernels: none -> 82.5 us  [body(): pl.pallas_call(run, out_shape=(state_out, state_out, state_out, jax.Shape...]
    dot_general x9 -> x0, matrix products: 8.97 us -> none  [the longest x1 2.61 us: body(): weight_part = jnp.dot(pooled.T, d_proj, precision=highest)]
  transfers between devices with their start and end apart: 2 -> 0, of which waited for: 2 -> 0; matrix products, arithmetic and copies ran while one was open for 1% -> 0% of each run, Pallas kernels for 0% -> 0%
where the time goes in v1:
time: 94 us; the launch traced here: 93.2 us
  Pallas kernels  82.5 us (88%)
  local copies, waits for them, and re-layouts  8.23 us (9%)
  between operations  2.46 us (3%)
    pallas_call x1, Pallas kernels, body(): pl.pallas_call(run, out_shape=(state_out, state_out, state_out, jax.Shape...  82.5 us
    unnamed x25, local copies, waits for them, and re-layouts  8.23 us

profile of v1, /device:TPU:1, one launch (start us, length us, event | category | flops | bytes accessed | tf_op | source)
XLA Modules:
  0.0 93.2 jit_solution(11894775753483159887)
XLA Ops:
  0.6 0.0 copy-start.6
  0.6 0.0 copy-start.5
  0.7 0.0 copy-start.4
  0.7 0.0 copy-start.7
  0.7 0.0 copy-start.8
  0.7 0.0 copy-start.9
  0.7 0.6 copy-done.6
  1.3 0.0 copy-done.5
  1.3 0.0 copy-done.4
  1.3 0.0 copy-done.7
  1.4 0.0 copy-done.8
  1.4 0.0 copy-done.9
  1.4 0.0 copy-start
  1.4 1.1 %copy-done = bf16[512,768]{1,0:T(8,128)(2,1)S(1)} copy-done((bf16[512,768]{1,0:T(8,128)(2,1)S(1)}, bf16[512,768]{1,0:T(8,128)(2,1)}, u32[]{:S(2)}) %copy-start) | copy-done | bytes 786456
  2.5 0.0 copy-start.1
  2.5 0.9 %copy-done.1 = bf16[4,64,512]{2,1,0:T(8,128)(2,1)S(1)} copy-done((bf16[4,64,512]{2,1,0:T(8,128)(2,1)S(1)}, bf16[4,64,512]{2,1,0:T(8,128)(2,1)}, u32[]{:S(2)}) %copy-start.1) | copy-done | bytes 262168
  3.5 0.0 copy-start.2
  3.5 0.9 %copy-done.2 = bf16[4,64,512]{2,1,0:T(8,128)(2,1)S(1)} copy-done((bf16[4,64,512]{2,1,0:T(8,128)(2,1)S(1)}, bf16[4,64,512]{2,1,0:T(8,128)(2,1)}, u32[]{:S(2)}) %copy-start.2) | copy-done | bytes 262168
  4.4 0.0 copy-start.3
  4.4 0.9 %copy-done.3 = bf16[4,64,512]{2,1,0:T(8,128)(2,1)S(1)} copy-done((bf16[4,64,512]{2,1,0:T(8,128)(2,1)S(1)}, bf16[4,64,512]{2,1,0:T(8,128)(2,1)}, u32[]{:S(2)}) %copy-start.3) | copy-done | bytes 262168
  5.4 82.5 %shard_map.145 = (bf16[256,512]{1,0:T(8,128)(2,1)S(1)}, bf16[256,512]{1,0:T(8,128)(2,1)S(1)}, bf16[256,512]{1,0:T(8,128)(2,1)S(1)}, bf16[512,768]{1,0:T(8,128)(2...) custom-call(bf16[256,512]{1,0:T(8,128)(2,1)S(1)} %bitcast.9, bf16[256,512]{1,0:T(8,128)(2,1)S(1)} %bitcast.10, ...), custom_call_target="tpu_custom_call" | custom-call | tf_op jit(solution)/shard_map/pallas_call | solution.py:341
  87.8 0.7 copy.22
  88.5 0.7 copy.23
  89.2 0.7 copy.24
  89.9 0.9 copy.25
  90.8 0.6 copy.26
Async XLA Ops:
  0.6 0.7 copy-start.6
  0.6 0.7 copy-start.5
  0.7 0.7 copy-start.4
  0.7 0.7 copy-start.7
  0.7 0.7 copy-start.8
  0.7 0.7 copy-start.9
  1.4 1.1 %copy-start = (bf16[512,768]{1,0:T(8,128)(2,1)S(1)}, bf16[512,768]{1,0:T(8,128)(2,1)}, u32[]{:S(2)}) copy-start(bf16[512,768]{1,0:T(8,128)(2,1)} %w_ref.1) | copy-start | bytes 2359300
  2.5 0.9 %copy-start.1 = (bf16[4,64,512]{2,1,0:T(8,128)(2,1)S(1)}, bf16[4,64,512]{2,1,0:T(8,128)(2,1)}, u32[]{:S(2)}) copy-start(bf16[4,64,512]{2,1,0:T(8,128)(2,1)} %param.10) | copy-start | bytes 786436
  3.5 0.9 %copy-start.2 = (bf16[4,64,512]{2,1,0:T(8,128)(2,1)S(1)}, bf16[4,64,512]{2,1,0:T(8,128)(2,1)}, u32[]{:S(2)}) copy-start(bf16[4,64,512]{2,1,0:T(8,128)(2,1)} %param.11) | copy-start | bytes 786436
  4.4 0.9 %copy-start.3 = (bf16[4,64,512]{2,1,0:T(8,128)(2,1)S(1)}, bf16[4,64,512]{2,1,0:T(8,128)(2,1)}, u32[]{:S(2)}) copy-start(bf16[4,64,512]{2,1,0:T(8,128)(2,1)} %param.12) | copy-start | bytes 786436

commit v2 on v1

--- a/solution.py
+++ b/solution.py
@@ -27,6 +27,7 @@
 bf16 = jnp.bfloat16
 NN = (((1,), (0,)), ((), ()))
 NTD = (((1,), (1,)), ((), ()))
+TN = (((0,), (0,)), ((), ()))
 
 
 def dot(a, b, dims=NN):
@@ -58,17 +59,30 @@
 
 
 def kernel(
-    x_refs,
-    len_refs,
+    x_hbm,
+    len_hbm,
+    gain_hbm,
+    w_hbm,
+    owner_hbm,
+    slot_hbm,
+    lifted_hbm,
+    factors_hbm,
+    gw_hbm,
+    gg_hbm,
+    loss_hbm,
+    xs,
+    lifted_ref,
+    factors_ref,
+    gw_ref,
+    gg_ref,
+    loss_ref,
+    s_out_copy,
+    len_ref,
     gain_ref,
     w_ref,
     owner_ref,
     slot_ref,
-    g_refs,
-    gw_ref,
-    gg_ref,
-    loss_ref,
-    xs,
+    s_in_copy,
     sq_own,
     sq_land,
     dot_own,
@@ -138,6 +152,29 @@
         cp.start()
         return cp
 
+    loads = []
+
+    def load(src, dst):
+        cp = pltpu.make_async_copy(src, dst, s_in_copy.at[len(loads)])
+        cp.start()
+        loads.append(cp)
+
+    for i in range(KINDS):
+        load(x_hbm[i], xs.at[pl.ds(i * SLOTS * LEN, SLOTS * LEN), :])
+    for i in range(KINDS):
+        load(len_hbm[i], len_ref.at[i])
+    load(gain_hbm, gain_ref)
+    load(owner_hbm, owner_ref)
+    load(slot_hbm, slot_ref)
+    load(w_hbm, w_ref)
+
+    stores = []
+
+    def store(src, dst):
+        cp = pltpu.make_async_copy(src, dst, s_out_copy.at[len(stores)])
+        cp.start()
+        stores.append(cp)
+
     barrier = pltpu.get_barrier_semaphore()
     greeted = (
         [tensor_peer(k) for k in range(1, NT)]
@@ -147,18 +184,23 @@
     for peer in greeted:
         pl.semaphore_signal(barrier, inc=1, device_id=peer, device_id_type=MESH)
 
-    for i in range(KINDS):
-        xs[pl.ds(i * SLOTS * LEN, SLOTS * LEN), :] = x_refs[i][...]
+    for cp in loads[:KINDS]:
+        cp.wait()
     xf = xs[...].astype(f32)
     xf = xf * xf
     part = (xf[:, 0:128] + xf[:, 128:256]) + (xf[:, 256:384] + xf[:, 384:512])
     sq_own[...] = exact_dot(jnp.ones((8, 128), f32), part, NTD)[0:1]
 
+    for cp in loads[KINDS:]:
+        cp.wait()
     pl.semaphore_wait(barrier, len(greeted))
 
-    def tensor_sum(own, land, ss, rs):
+    def tensor_send(own, land, ss, rs):
         cps = [send(own, land.at[t], ss.at[k - 1], rs.at[k - 1], tensor_peer(k)) for k in range(1, NT)]
         land[t] = own[...]
+        return cps
+
+    def tensor_sum(cps, land):
         for cp in cps:
             cp.wait()
         total = land[0]
@@ -166,20 +208,22 @@
             total = total + land[i]
         return total
 
-    squares = tensor_sum(sq_own, sq_land, s_sq, r_sq)
+    squares = tensor_sum(tensor_send(sq_own, sq_land, s_sq, r_sq), sq_land)
     scales = lax.rsqrt(squares / D + epsilon)
     lane = lax.broadcasted_iota(jnp.int32, (1, TOK), 1)
     seq = lane // LEN
     lens = jnp.zeros((1, TOK), jnp.int32)
     for i in range(KINDS):
         for s in range(SLOTS):
-            lens = jnp.where(seq == i * SLOTS + s, len_refs[i][s], lens)
+            lens = jnp.where(seq == i * SLOTS + s, len_ref[i, s], lens)
     live = jnp.where(lane % LEN < lens, 1.0 / lens.astype(f32), 0.0)
     coeffs = scales * live
     row = lax.broadcasted_iota(jnp.int32, (16, TOK), 0)
     mine = (row % 4) * SLOTS + row // 4 == seq
     plain = join3(dot(split3(jnp.where(mine, coeffs, 0.0)), xs[...]))
-    PB[x, z] = plain
+    for s in range(SLOTS):
+        for k in range(KINDS):
+            PB[x, z, k, s : s + 1, :] = plain[4 * s + k : 4 * s + k + 1]
     px = [
         send(PB.at[x, z], PB.at[x, z], s_px.at[k - 1], r_px.at[k - 1], x_peer(k))
         for k in range(1, NX)
@@ -204,10 +248,13 @@
     for i in range(1, NT):
         piece = piece + rs_land[i]
     place = lax.broadcasted_iota(jnp.int32, (4, H), 0)
-    at = (b * 4 + a) * NZ + z
-    L[c, at] = jnp.where(place == 3, ids_ref[y], piece)
-
-    zs = [send(L.at[c, at], L.at[c, at], s_z.at[k - 1], r_z.at[k - 1], z_peer(k)) for k in range(1, NZ)]
+    L[c, 0, b, a, 4] = jnp.where(place == 3, ids_ref[y], piece)
+    mine_block = L.at[c, 0, b, a, 4]
+
+    zs = {}
+    for k in (8, 9, 7, 10, 6, 11, 5, 12, 4, 13, 3, 14, 2, 15, 1):
+        rel = (4 - k) % NZ
+        zs[rel] = send(mine_block, L.at[c, rel // 8, b, a, rel % 8], s_z.at[k - 1], r_z.at[k - 1], z_peer(k))
 
     for cp in px:
         cp.wait()
@@ -222,47 +269,69 @@
             out.append(send(down, down, s_pz.at[1, step - 1], r_pz.at[1, step - 1], z_peer(NZ - 1)))
         return out
 
-    turn = ring(1)
-
     def next_turn(turn, step):
         for cp in turn:
             cp.wait()
         return ring(step)
 
-    for cp in zs:
-        cp.wait()
-    line = L.at[c, pl.ds((b * 4 + a) * NZ, NZ)]
-    cps = [send(line, line, s_a.at[k - 1], r_a.at[k - 1], a_peer(k)) for k in range(1, 4)]
+    def along_a(g):
+        line = L.at[c, g, b, a]
+        return [send(line, line, s_a.at[g, k - 1], r_a.at[g, k - 1], a_peer(k)) for k in (2, 1, 3)]
+
+    def along_b(g):
+        plane = L.at[c, g, b]
+        cps = [send(plane, plane, s_b.at[g, k - 1], r_b.at[g, k - 1], b_peer(k)) for k in (2, 1, 3)]
+        return cps, send(plane, plane, s_c.at[g, 0], r_c.at[g, 0], sibling)
+
+    def across(g, k):
+        got = L.at[c, g, (b + 4 - k) % 4]
+        return send(got, got, s_c.at[g, k], r_c.at[g, k], sibling)
+
+    turn = ring(1)
+    for rel in (5, 3, 6, 2, 7, 1, 0):
+        zs[rel].wait()
+    a0 = along_a(0)
     turn = next_turn(turn, 2)
-    for cp in cps:
-        cp.wait()
-    plane = L.at[c, pl.ds(b * 64, 64)]
-    cps = [send(plane, plane, s_b.at[k - 1], r_b.at[k - 1], b_peer(k)) for k in range(1, 4)]
-    across = [send(plane, plane, s_c.at[0], r_c.at[0], sibling)]
+    for rel in range(8, 16):
+        zs[rel].wait()
+    a1 = along_a(1)
+    for cp in a0:
+        cp.wait()
+    b0, over = along_b(0)
+    crossing = [over]
     turn = next_turn(turn, 3)
+    for cp in a1:
+        cp.wait()
+    b1, over = along_b(1)
+    crossing.append(over)
+    turn = next_turn(turn, 4)
     for k in (1, 3, 2):
-        cps[k - 1].wait()
-        got = L.at[c, pl.ds(((b + 4 - k) % 4) * 64, 64)]
-        across.append(send(got, got, s_c.at[k], r_c.at[k], sibling))
-        turn = next_turn(turn, {1: 4, 3: 5, 2: 6}[k])
-    for cp in across:
-        cp.wait()
-
+        b0[(2, 1, 3).index(k)].wait()
+        crossing.append(across(0, k))
+    turn = next_turn(turn, 5)
+    for k in (1, 3, 2):
+        b1[(2, 1, 3).index(k)].wait()
+        crossing.append(across(1, k))
+    turn = next_turn(turn, 6)
+    for cp in crossing:
+        cp.wait()
+    turn = next_turn(turn, 7)
+
+    shift = (z + NZ - 4) % NZ
     for k in range(KINDS):
         for s in range(SLOTS):
-            left = L[0, pl.ds(s * 64, 64), k, :]
-            right = jnp.concatenate(
-                [L[1, pl.ds(i * 64 + s * NZ, NZ), k, :] for i in range(NX)], 0
-            )
-            dproj[pl.ds(k * ALL + s * DP, DP), pl.ds(0, H)] = left
-            dproj[pl.ds(k * ALL + s * DP, DP), pl.ds(H, H)] = right
+            for i in range(NX):
+                left = jnp.concatenate([L[0, g, s, i, :, k, :] for g in range(2)], 0)
+                right = jnp.concatenate([L[1, g, i, s, :, k, :] for g in range(2)], 0)
+                rows = pl.ds(k * ALL + s * DP + i * NZ, NZ)
+                dproj[rows, :] = pltpu.roll(jnp.concatenate([left, right], 1), shift, 0)
     projs = dproj[...]
     r_norm = lax.rsqrt(jnp.sum(projs * projs, -1, keepdims=True) + epsilon)
     unit = projs * r_norm
     hi, lo = split2(unit)
     u_hi[...] = hi
     u_lo[...] = lo
-    turn = next_turn(turn, 7)
+    turn = next_turn(turn, 8)
 
     def part_of(k):
         rows = pl.ds(k * ALL, ALL)
@@ -273,7 +342,14 @@
     s_neg = score_scale * dot3(uq, un, NTD)
     lanes = lax.broadcasted_iota(jnp.int32, (ALL, ALL), 1)
     diag = lax.broadcasted_iota(jnp.int32, (ALL, ALL), 0) == lanes
-    all_ids = L[0, :, 3, 0:128].astype(jnp.int32)
+    all_ids = jnp.concatenate(
+        [
+            pltpu.roll(jnp.concatenate([L[0, g, s, i, :, 3, 0:128] for g in range(2)], 0), shift, 0)
+            for s in range(SLOTS)
+            for i in range(NX)
+        ],
+        0,
+    ).astype(jnp.int32)
     named = lanes == all_ids[:, 0:1]
     for k in range(1, NEGS):
         named = jnp.logical_or(named, lanes == all_ids[:, k : k + 1])
@@ -282,10 +358,10 @@
     total = jnp.sum(ex_in, 1, keepdims=True) + jnp.sum(ex_neg, 1, keepdims=True)
     own_score = jnp.sum(jnp.where(diag, s_in, 0.0), 1, keepdims=True)
     loss_ref[...] = jnp.sum(jnp.log(total) - own_score, 0, keepdims=True) / ALL
+    store(loss_ref, loss_hbm)
     factor = (score_scale * loss_scale) / total
     g_in = ex_in * factor - jnp.where(diag, score_scale * loss_scale, 0.0)
     g_neg = ex_neg * factor
-    turn = next_turn(turn, 8)
     d_uq = dot3(split2(g_in), up) + dot3(split2(g_neg), un)
     d_up = dot3(split2(g_in.T), uq)
     d_un = dot3(split2(g_neg.T), uq)
@@ -298,60 +374,117 @@
             own_rows[4 * s + k : 4 * s + k + 1, :] = dproj[pl.ds(k * ALL + s * DP + dp, 1), :]
     d_pooled = join3(dot(split3(own_rows[...]), w_ref[...], NTD))
     lifted = d_pooled * gain
+    lifted_ref[...] = lifted
+    store(lifted_ref, lifted_hbm)
     spread = join3(dot(split3(lifted), xs[...], NTD))
     dot_own[...] = jnp.sum(jnp.where(mine, spread, 0.0), 0, keepdims=True)
+    dots_sent = tensor_send(dot_own, dot_land, s_dot, r_dot)
     for cp in turn:
         cp.wait()
-    dots = tensor_sum(dot_own, dot_land, s_dot, r_dot)
-
-    inner = scales * scales / D * dots
-    rows = jnp.concatenate([coeffs, coeffs * inner, jnp.zeros((6, TOK), f32)], 0)
-    cols = rows.T
-    for i in range(KINDS):
-        for s in range(SLOTS):
-            at = (i * SLOTS + s) * LEN
-            value = cols[at : at + LEN, 0:1] * lifted[4 * s + i : 4 * s + i + 1, :] - (
-                xs[pl.ds(at, LEN), :].astype(f32) * cols[at : at + LEN, 1:2]
-            )
-            g_refs[i][pl.ds(s * LEN, LEN), :] = value.astype(bf16)
 
     plain_all = jnp.concatenate(
         [
-            jnp.concatenate([PB[i, :, 4 * s + k, :] for i in range(NX)], 0)
+            PB[i, :, k, s, :]
             for k in range(KINDS)
             for s in range(SLOTS)
+            for i in range(NX)
         ],
         0,
     )
-    grad = dot3(split2(plain_all.T), split2(dproj[...])) / loss_scale
-    gg_ref[...] = exact_dot(jnp.ones((8, E), f32), grad * w_ref[...].astype(f32), NTD)[0:1]
+    grad = dot3(split2(plain_all), split2(dproj[...]), TN) / loss_scale
+    weighted = grad * w_ref[...].astype(f32)
+    fold = weighted[:, 0:128]
+    for i in range(1, E // 128):
+        fold = fold + weighted[:, i * 128 : (i + 1) * 128]
+    gg_ref[...] = exact_dot(jnp.ones((8, 128), f32), fold, NTD)[0:1]
     gw_ref[...] = (grad * gain.T).astype(bf16)
+    store(gg_ref, gg_hbm)
+    store(gw_ref, gw_hbm)
+
+    dots = tensor_sum(dots_sent, dot_land)
+
+    inner = scales * scales / D * dots
+    factors_ref[...] = jnp.concatenate([coeffs, coeffs * inner, jnp.zeros((6, TOK), f32)], 0)
+    store(factors_ref, factors_hbm)
+    for cp in stores:
+        cp.wait()
+
+
+def finish_kernel(*refs):
+    x_hbm, (lifted_hbm, factors_hbm, gw_in, gg_in, loss_in) = refs[0:3], refs[3:8]
+    g_hbm, (gw_out, gg_out, loss_out) = refs[8:11], refs[11:14]
+    xs, gs, lifted_ref, factors_ref, gw_ref, gg_ref, loss_ref, s_load, s_store = refs[14:]
+
+    def copy(src, dst, sem):
+        cp = pltpu.make_async_copy(src, dst, sem)
+        cp.start()
+        return cp
+
+    def part(ref, i):
+        return ref.at[pl.ds(i * SLOTS * LEN, SLOTS * LEN), :]
+
+    first = [copy(factors_hbm, factors_ref, s_load.at[0]), copy(lifted_hbm, lifted_ref, s_load.at[1])]
+    states = [copy(x_hbm[i], part(xs, i), s_load.at[2 + i]) for i in range(KINDS)]
+    passed = [
+        (copy(src, mid, s_load.at[5 + i]), mid, dst)
+        for i, (src, mid, dst) in enumerate(
+            ((gw_in, gw_ref, gw_out), (gg_in, gg_ref, gg_out), (loss_in, loss_ref, loss_out))
+        )
+    ]
+    for cp in first:
+        cp.wait()
+    cols = factors_ref[...].T
+    stores = []
+    for i in range(KINDS):
+        states[i].wait()
+        for s in range(SLOTS):
+            at = (i * SLOTS + s) * LEN
+            value = cols[at : at + LEN, 0:1] * lifted_ref[4 * s + i : 4 * s + i + 1, :] - (
+                xs[pl.ds(at, LEN), :].astype(f32) * cols[at : at + LEN, 1:2]
+            )
+            gs[pl.ds(at, LEN), :] = value.astype(bf16)
+        stores.append(copy(part(gs, i), g_hbm[i], s_store.at[i]))
+        cp, mid, dst = passed[i]
+        cp.wait()
+        stores.append(copy(mid, dst, s_store.at[KINDS + i]))
+    for cp in stores:
+        cp.wait()
 
 
 def body(q, p, n, q_len, p_len, n_len, gain, w, owner, slot):
-    vmem = pl.BlockSpec(memory_space=pltpu.VMEM)
-    smem = pl.BlockSpec(memory_space=pltpu.SMEM)
+    hbm = pl.BlockSpec(memory_space=pltpu.HBM)
     dma = pltpu.SemaphoreType.DMA
     states = [v.reshape(SLOTS * LEN, F) for v in (q, p, n)]
 
-    def run(x0, x1, x2, l0, l1, l2, gain_ref, w_ref, owner_ref, slot_ref, g0, g1, g2, *rest):
-        kernel((x0, x1, x2), (l0, l1, l2), gain_ref, w_ref, owner_ref, slot_ref, (g0, g1, g2), *rest)
+    def run(x0, x1, x2, l0, l1, l2, *rest):
+        kernel((x0, x1, x2), (l0, l1, l2), *rest)
 
     state_out = jax.ShapeDtypeStruct((SLOTS * LEN, F), bf16)
-    g0, g1, g2, gw, gg, loss = pl.pallas_call(
+    results = pl.pallas_call(
         run,
         out_shape=(
-            state_out,
-            state_out,
-            state_out,
+            jax.ShapeDtypeStruct((16, F), f32),
+            jax.ShapeDtypeStruct((8, TOK), f32),
             jax.ShapeDtypeStruct((F, E), bf16),
             jax.ShapeDtypeStruct((1, F), f32),
             jax.ShapeDtypeStruct((1, 1), f32),
         ),
-        in_specs=[vmem] * 3 + [smem] * 3 + [vmem] * 4,
-        out_specs=(vmem,) * 6,
+        in_specs=[hbm] * 10,
+        out_specs=(hbm,) * 5,
         scratch_shapes=[
             pltpu.VMEM((TOK, F), bf16),
+            pltpu.VMEM((16, F), f32),
+            pltpu.VMEM((8, TOK), f32),
+            pltpu.VMEM((F, E), bf16),
+            pltpu.VMEM((1, F), f32),
+            pltpu.VMEM((1, 1), f32),
+            dma((5,)),
+            pltpu.SMEM((KINDS, SLOTS), jnp.int32),
+            pltpu.VMEM((1, F), f32),
+            pltpu.VMEM((F, E), bf16),
+            pltpu.VMEM((SLOTS, NEGS), jnp.int32),
+            pltpu.VMEM((SLOTS, NEGS), jnp.int32),
+            dma((10,)),
             pltpu.VMEM((1, TOK), f32),
             pltpu.VMEM((NT, 1, TOK), f32),
             pltpu.VMEM((1, TOK), f32),
@@ -359,8 +492,8 @@
             pltpu.VMEM((NT, 4, H), f32),
             pltpu.VMEM((NT, 4, H), f32),
             pltpu.VMEM((SLOTS, 1, H), f32),
-            pltpu.VMEM((NC, ALL, 4, H), f32),
-            pltpu.VMEM((NX, NZ, 16, F), f32),
+            pltpu.VMEM((NC, 2, 4, 4, 8, 4, H), f32),
+            pltpu.VMEM((NX, NZ, KINDS, SLOTS, F), f32),
             pltpu.VMEM((SEQ, E), bf16),
             pltpu.VMEM((SEQ, E), bf16),
             pltpu.VMEM((SEQ, E), f32),
@@ -371,12 +504,12 @@
             dma((NT - 1,)),
             dma((NZ - 1,)),
             dma((NZ - 1,)),
-            dma((3,)),
-            dma((3,)),
-            dma((3,)),
-            dma((3,)),
-            dma((4,)),
-            dma((4,)),
+            dma((2, 3)),
+            dma((2, 3)),
+            dma((2, 3)),
+            dma((2, 3)),
+            dma((2, 4)),
+            dma((2, 4)),
             dma((NT - 1,)),
             dma((NT - 1,)),
             dma((3,)),
@@ -385,9 +518,27 @@
             dma((2, 8)),
         ],
         compiler_params=pltpu.CompilerParams(
-            collective_id=0, has_side_effects=True, vmem_limit_bytes=50 << 20
+            collective_id=0, has_side_effects=True, vmem_limit_bytes=62 << 20
         ),
     )(*states, q_len, p_len, n_len, gain.reshape(1, F), w, owner, slot)
+    g0, g1, g2, gw, gg, loss = pl.pallas_call(
+        finish_kernel,
+        out_shape=(state_out,) * 3 + tuple(jax.ShapeDtypeStruct(v.shape, v.dtype) for v in results[2:]),
+        in_specs=[hbm] * 8,
+        out_specs=(hbm,) * 6,
+        scratch_shapes=[
+            pltpu.VMEM((TOK, F), bf16),
+            pltpu.VMEM((TOK, F), bf16),
+            pltpu.VMEM((16, F), f32),
+            pltpu.VMEM((8, TOK), f32),
+            pltpu.VMEM((F, E), bf16),
+            pltpu.VMEM((1, F), f32),
+            pltpu.VMEM((1, 1), f32),
+            dma((8,)),
+            dma((6,)),
+        ],
+        compiler_params=pltpu.CompilerParams(vmem_limit_bytes=62 << 20),
+    )(*states, *results)
     shape = q.shape
     return (
         g0.reshape(shape),

time: 94 us -> 74.5 us (0.79)
  Pallas kernels: 82.5 us -> 73.7 us
  local copies, waits for them, and re-layouts: 8.23 us -> 0 us
  between operations: 2.46 us -> 0.64 us
    pallas_call x1 -> x2, Pallas kernels: 82.5 us -> 73.7 us  [the longest x1 70.4 us: body(): pl.pallas_call(run, out_shape=(jax.ShapeDtypeStruct((16, F), f32), jax.Sh...]
    unnamed x25 -> x0, local copies, waits for them, and re-layouts: 8.23 us -> none
where the time goes in v2:
time: 74.5 us; the launch traced here: 74.3 us
  Pallas kernels  73.7 us (99%)
    pallas_call x1, Pallas kernels, body(): pl.pallas_call(run, out_shape=(jax.ShapeDtypeStruct((16, F), f32), jax.Sh...  70.4 us
    pallas_call x1, Pallas kernels, body(): pl.pallas_call(finish_kernel, out_shape=(state_out,) * 3 + tuple((jax.Sha...  3.25 us

profile of v2, /device:TPU:1, one launch (start us, length us, event | category | flops | bytes accessed | tf_op | source)
XLA Modules:
  0.0 74.3 jit_solution(10248222147038693298)
XLA Ops:
  0.6 70.4 %shard_map.145 = (f32[16,512]{1,0:T(8,128)}, f32[8,768]{1,0:T(8,128)}, bf16[512,768]{1,0:T(8,128)(2,1)}, f32[1,512]{1,0:T(1,128)}, f32[1,1]{1,0:T(1,128)}) custom-call(bf16[256,512]{1,0:T(8,128)(2,1)} %bitcast.9, bf16[256,512]{1,0:T(8,128)(2,1)} %bitcast.11, bf16[256,512]{1,0:T(8,128)(2,1)} %bitcast.13, s32[4]{0:T(128)} %l0.1, s32[4]{0:T(128)} %l1.1, s32[4]{0:T(128)} %l2.1, ...), custom_call_target="tpu_custom_call" | custom-call | tf_op jit(solution)/shard_map/pallas_call | solution.py:463
  71.0 3.3 %shard_map.146 = (bf16[256,512]{1,0:T(8,128)(2,1)}, bf16[256,512]{1,0:T(8,128)(2,1)}, bf16[256,512]{1,0:T(8,128)(2,1)}, bf16[512,768]{1,0:T(8,128)(2,1)}, f32[1,512]{1,0:T(1,128)}, /*index=5*/f32[1,1]{1,0:T(1,128)}) custom-call(bf16[256,512]{1,0:T(8,128)(2,1)} %bitcast.10, bf16[256,512]{1,0:T(8,128)(2,1)} %bitcast.12, bf16[256,512]{1,0:T(8,128)(2,1)} %bitcast.14, ...), custom_call_target="tpu_custom_call" | custom-call | tf_op jit(solution)/shard_map/pallas_call | solution.py:524

commit v3 on v2

--- a/solution.py
+++ b/solution.py
@@ -95,6 +95,7 @@
     u_hi,
     u_lo,
     dproj,
+    parts,
     own_rows,
     s_sq,
     r_sq,
@@ -223,11 +224,7 @@
     plain = join3(dot(split3(jnp.where(mine, coeffs, 0.0)), xs[...]))
     for s in range(SLOTS):
         for k in range(KINDS):
-            PB[x, z, k, s : s + 1, :] = plain[4 * s + k : 4 * s + k + 1]
-    px = [
-        send(PB.at[x, z], PB.at[x, z], s_px.at[k - 1], r_px.at[k - 1], x_peer(k))
-        for k in range(1, NX)
-    ]
+            PB[0, x, 4, k, s : s + 1, :] = plain[4 * s + k : 4 * s + k + 1]
     gain = gain_ref[...]
     proj = join3(dot(split3(plain * gain), w_ref[...]))
     for s in range(SLOTS):
@@ -238,6 +235,16 @@
         for k in range(1, NT)
     ]
     rs_land[t] = stage[t]
+
+    def pz_send(ks):
+        block = PB.at[0, x, 4]
+        out = []
+        for k in ks:
+            rel = (4 - k) % NZ
+            out.append(send(block, PB.at[rel // 8, x, rel % 8], s_pz.at[k - 1], r_pz.at[k - 1], z_peer(k)))
+        return out
+
+    pz0 = pz_send((4, 3, 13, 2, 14, 1, 15))
     ids = (slot_ref[...] * DP + owner_ref[...]).astype(f32)
     ids_ref[...] = jnp.zeros_like(ids_ref)
     for s in range(SLOTS):
@@ -256,66 +263,84 @@
         rel = (4 - k) % NZ
         zs[rel] = send(mine_block, L.at[c, rel // 8, b, a, rel % 8], s_z.at[k - 1], r_z.at[k - 1], z_peer(k))
 
-    for cp in px:
-        cp.wait()
-
-    def ring(step):
-        out = []
-        if step <= 8:
-            up = PB.at[:, (z - step + 1 + NZ) % NZ]
-            out.append(send(up, up, s_pz.at[0, step - 1], r_pz.at[0, step - 1], z_peer(1)))
-        if step <= 7:
-            down = PB.at[:, (z + step - 1) % NZ]
-            out.append(send(down, down, s_pz.at[1, step - 1], r_pz.at[1, step - 1], z_peer(NZ - 1)))
-        return out
-
-    def next_turn(turn, step):
-        for cp in turn:
+    def px_send(g, i, block, k):
+        return send(block, block, s_px.at[g, i], r_px.at[g, i], x_peer(k))
+
+    def px_start(g, pz):
+        for cp in pz:
             cp.wait()
-        return ring(step)
+        return [px_send(g, 0, PB.at[g, x], 1), px_send(g, 1, PB.at[g, x], 3)]
+
+    def px_relay(g, cps):
+        cps[0].wait()
+        cps.append(px_send(g, 2, PB.at[g, (x + 3) % NX, pl.ds(0, 4)], 1))
+        cps[1].wait()
+        cps.append(px_send(g, 3, PB.at[g, (x + 1) % NX, pl.ds(4, 4)], 3))
 
     def along_a(g):
         line = L.at[c, g, b, a]
         return [send(line, line, s_a.at[g, k - 1], r_a.at[g, k - 1], a_peer(k)) for k in (2, 1, 3)]
 
-    def along_b(g):
-        plane = L.at[c, g, b]
-        cps = [send(plane, plane, s_b.at[g, k - 1], r_b.at[g, k - 1], b_peer(k)) for k in (2, 1, 3)]
-        return cps, send(plane, plane, s_c.at[g, 0], r_c.at[g, 0], sibling)
-
-    def across(g, k):
-        got = L.at[c, g, (b + 4 - k) % 4]
-        return send(got, got, s_c.at[g, k], r_c.at[g, k], sibling)
-
-    turn = ring(1)
+    def half(g, k, h):
+        return L.at[c, g, (b + k) % 4, pl.ds(2 * h, 2)]
+
+    def b_send(g, i, block, k):
+        return send(block, block, s_b.at[g, i], r_b.at[g, i], b_peer(k))
+
+    def cross(g, k):
+        plane = L.at[c, g, (b + k) % 4]
+        return send(plane, plane, s_c.at[g, k], r_c.at[g, k], sibling)
+
+    def b_start(g):
+        cps = [
+            b_send(g, 0, half(g, 0, 0), 1),
+            b_send(g, 1, half(g, 0, 1), 3),
+            b_send(g, 2, half(g, 0, 1), 1),
+            b_send(g, 3, half(g, 0, 0), 3),
+        ]
+        return cps, [cross(g, 0)]
+
+    def b_relay(g, cps):
+        cps[0].wait()
+        cps.append(b_send(g, 4, half(g, 3, 0), 1))
+        cps[1].wait()
+        cps.append(b_send(g, 5, half(g, 1, 1), 3))
+
+    def b_middle(g, cps, over):
+        cps[2].wait()
+        over.append(cross(g, 3))
+        cps[3].wait()
+        over.append(cross(g, 1))
+
+    def b_end(g, cps, over):
+        cps[4].wait()
+        cps[5].wait()
+        over.append(cross(g, 2))
+
+    px0 = px_start(0, pz0)
     for rel in (5, 3, 6, 2, 7, 1, 0):
         zs[rel].wait()
     a0 = along_a(0)
-    turn = next_turn(turn, 2)
+    pz1 = pz_send((8, 9, 7, 10, 6, 11, 5, 12))
     for rel in range(8, 16):
         zs[rel].wait()
     a1 = along_a(1)
+    px_relay(0, px0)
     for cp in a0:
         cp.wait()
-    b0, over = along_b(0)
-    crossing = [over]
-    turn = next_turn(turn, 3)
+    b0, over0 = b_start(0)
     for cp in a1:
         cp.wait()
-    b1, over = along_b(1)
-    crossing.append(over)
-    turn = next_turn(turn, 4)
-    for k in (1, 3, 2):
-        b0[(2, 1, 3).index(k)].wait()
-        crossing.append(across(0, k))
-    turn = next_turn(turn, 5)
-    for k in (1, 3, 2):
-        b1[(2, 1, 3).index(k)].wait()
-        crossing.append(across(1, k))
-    turn = next_turn(turn, 6)
-    for cp in crossing:
-        cp.wait()
-    turn = next_turn(turn, 7)
+    b1, over1 = b_start(1)
+    b_relay(0, b0)
+    b_middle(0, b0, over0)
+    b_relay(1, b1)
+    b_end(0, b0, over0)
+    b_middle(1, b1, over1)
+    b_end(1, b1, over1)
+    px1 = px_start(1, pz1)
+    for cp in over0 + over1:
+        cp.wait()
 
     shift = (z + NZ - 4) % NZ
     for k in range(KINDS):
@@ -331,7 +356,6 @@
     hi, lo = split2(unit)
     u_hi[...] = hi
     u_lo[...] = lo
-    turn = next_turn(turn, 8)
 
     def part_of(k):
         rows = pl.ds(k * ALL, ALL)
@@ -368,6 +392,8 @@
     d_unit = jnp.concatenate([d_uq, d_up, d_un], 0)
     dproj[...] = (d_unit - unit * jnp.sum(unit * d_unit, -1, keepdims=True)) * r_norm
 
+    px_relay(1, px1)
+
     own_rows[...] = jnp.zeros_like(own_rows)
     for s in range(SLOTS):
         for k in range(KINDS):
@@ -379,19 +405,32 @@
     spread = join3(dot(split3(lifted), xs[...], NTD))
     dot_own[...] = jnp.sum(jnp.where(mine, spread, 0.0), 0, keepdims=True)
     dots_sent = tensor_send(dot_own, dot_land, s_dot, r_dot)
-    for cp in turn:
-        cp.wait()
-
-    plain_all = jnp.concatenate(
-        [
-            PB[i, :, k, s, :]
-            for k in range(KINDS)
-            for s in range(SLOTS)
-            for i in range(NX)
-        ],
-        0,
-    )
-    grad = dot3(split2(plain_all), split2(dproj[...]), TN) / loss_scale
+
+    def line_part(i):
+        plains = jnp.concatenate(
+            [
+                pltpu.roll(jnp.concatenate([PB[g, i, :, k, s, :] for g in range(2)], 0), shift, 0)
+                for k in range(KINDS)
+                for s in range(SLOTS)
+            ],
+            0,
+        )
+        projs = jnp.concatenate(
+            [
+                dproj[pl.ds(pl.multiple_of(k * ALL + s * DP + i * NZ, NZ), NZ), :]
+                for k in range(KINDS)
+                for s in range(SLOTS)
+            ],
+            0,
+        )
+        parts[i] = dot3(split2(plains), split2(projs), TN)
+
+    for k in (0, 1, 3):
+        line_part((x + k) % NX)
+    for cp in px0[2:] + px1[2:]:
+        cp.wait()
+    line_part((x + 2) % NX)
+    grad = ((parts[0] + parts[1]) + (parts[2] + parts[3])) / loss_scale
     weighted = grad * w_ref[...].astype(f32)
     fold = weighted[:, 0:128]
     for i in range(1, E // 128):
@@ -493,10 +532,11 @@
             pltpu.VMEM((NT, 4, H), f32),
             pltpu.VMEM((SLOTS, 1, H), f32),
             pltpu.VMEM((NC, 2, 4, 4, 8, 4, H), f32),
-            pltpu.VMEM((NX, NZ, KINDS, SLOTS, F), f32),
+            pltpu.VMEM((2, NX, 8, KINDS, SLOTS, F), f32),
             pltpu.VMEM((SEQ, E), bf16),
             pltpu.VMEM((SEQ, E), bf16),
             pltpu.VMEM((SEQ, E), f32),
+            pltpu.VMEM((NX, F, E), f32),
             pltpu.VMEM((16, E), f32),
             dma((NT - 1,)),
             dma((NT - 1,)),
@@ -506,16 +546,16 @@
             dma((NZ - 1,)),
             dma((2, 3)),
             dma((2, 3)),
-            dma((2, 3)),
-            dma((2, 3)),
+            dma((2, 6)),
+            dma((2, 6)),
             dma((2, 4)),
             dma((2, 4)),
             dma((NT - 1,)),
             dma((NT - 1,)),
-            dma((3,)),
-            dma((3,)),
-            dma((2, 8)),
-            dma((2, 8)),
+            dma((2, 4)),
+            dma((2, 4)),
+            dma((NZ - 1,)),
+            dma((NZ - 1,)),
         ],
         compiler_params=pltpu.CompilerParams(
             collective_id=0, has_side_effects=True, vmem_limit_bytes=62 << 20

time: 74.5 us -> 68 us (0.913)
  Pallas kernels: 73.7 us -> 67.2 us
    pallas_call x1, Pallas kernels: 70.4 us -> 63.9 us  [body(): pl.pallas_call(run, out_shape=(jax.ShapeDtypeStruct((16, F), f32), jax.Sh...]
where the time goes in v3:
time: 68 us; the launch traced here: 67.8 us
  Pallas kernels  67.2 us (99%)
    pallas_call x1, Pallas kernels, body(): pl.pallas_call(run, out_shape=(jax.ShapeDtypeStruct((16, F), f32), jax.Sh...  63.9 us
    pallas_call x1, Pallas kernels, body(): pl.pallas_call(finish_kernel, out_shape=(state_out,) * 3 + tuple((jax.Sha...  3.25 us

profile of v3, /device:TPU:1, one launch (start us, length us, event | category | flops | bytes accessed | tf_op | source)
XLA Modules:
  0.0 67.8 jit_solution(13483533178350737836)
XLA Ops:
  0.6 63.9 %shard_map.145 = (f32[16,512]{1,0:T(8,128)}, f32[8,768]{1,0:T(8,128)}, bf16[512,768]{1,0:T(8,128)(2,1)}, f32[1,512]{1,0:T(1,128)}, f32[1,1]{1,0:T(1,128)}) custom-call(bf16[256,512]{1,0:T(8,128)(2,1)} %bitcast.9, bf16[256,512]{1,0:T(8,128)(2,1)} %bitcast.11, bf16[256,512]{1,0:T(8,128)(2,1)} %bitcast.13, s32[4]{0:T(128)} %l0.1, s32[4]{0:T(128)} %l1.1, s32[4]{0:T(128)} %l2.1, ...), custom_call_target="tpu_custom_call" | custom-call | tf_op jit(solution)/shard_map/pallas_call | solution.py:502
  64.6 3.3 %shard_map.146 = (bf16[256,512]{1,0:T(8,128)(2,1)}, bf16[256,512]{1,0:T(8,128)(2,1)}, bf16[256,512]{1,0:T(8,128)(2,1)}, bf16[512,768]{1,0:T(8,128)(2,1)}, f32[1,512]{1,0:T(1,128)}, /*index=5*/f32[1,1]{1,0:T(1,128)}) custom-call(bf16[256,512]{1,0:T(8,128)(2,1)} %bitcast.10, bf16[256,512]{1,0:T(8,128)(2,1)} %bitcast.12, bf16[256,512]{1,0:T(8,128)(2,1)} %bitcast.14, ...), custom_call_target="tpu_custom_call" | custom-call | tf_op jit(solution)/shard_map/pallas_call | solution.py:564

commit v4 on v3

--- a/solution.py
+++ b/solution.py
@@ -83,6 +83,7 @@
     owner_ref,
     slot_ref,
     s_in_copy,
+    inside,
     sq_own,
     sq_land,
     dot_own,
@@ -180,20 +181,22 @@
     greeted = (
         [tensor_peer(k) for k in range(1, NT)]
         + [x_peer(k) for k in range(1, NX)]
-        + [z_peer(k) for k in range(1, NZ)]
+        + [z_peer(k) for k in (1, 2, NZ - 2, NZ - 1)]
     )
     for peer in greeted:
         pl.semaphore_signal(barrier, inc=1, device_id=peer, device_id_type=MESH)
 
-    for cp in loads[:KINDS]:
-        cp.wait()
-    xf = xs[...].astype(f32)
-    xf = xf * xf
-    part = (xf[:, 0:128] + xf[:, 128:256]) + (xf[:, 256:384] + xf[:, 384:512])
-    sq_own[...] = exact_dot(jnp.ones((8, 128), f32), part, NTD)[0:1]
-
-    for cp in loads[KINDS:]:
-        cp.wait()
+    ones = jnp.ones((16, 128), bf16)
+    for i in range(KINDS):
+        loads[i].wait()
+        tokens = pl.ds(i * SLOTS * LEN, SLOTS * LEN)
+        xf = xs[tokens, :].astype(f32)
+        xf = xf * xf
+        part = (xf[:, 0:128] + xf[:, 128:256]) + (xf[:, 256:384] + xf[:, 384:512])
+        sums = dot(ones, split3(part), NTD)[0:1]
+        n = SLOTS * LEN
+        sq_own[:, tokens] = (sums[:, 0:n] + sums[:, n : 2 * n]) + sums[:, 2 * n : 3 * n]
+
     pl.semaphore_wait(barrier, len(greeted))
 
     def tensor_send(own, land, ss, rs):
@@ -209,7 +212,17 @@
             total = total + land[i]
         return total
 
-    squares = tensor_sum(tensor_send(sq_own, sq_land, s_sq, r_sq), sq_land)
+    def greet(i, k):
+        for peer in (z_peer(k), z_peer(NZ - k)):
+            pl.semaphore_signal(inside.at[i], inc=1, device_id=peer, device_id_type=MESH)
+
+    squares_sent = tensor_send(sq_own, sq_land, s_sq, r_sq)
+    greet(0, 2)
+    for cp in loads[KINDS:]:
+        cp.wait()
+    squares = tensor_sum(squares_sent, sq_land)
+    pl.semaphore_wait(inside.at[0], 2)
+    greet(1, 4)
     scales = lax.rsqrt(squares / D + epsilon)
     lane = lax.broadcasted_iota(jnp.int32, (1, TOK), 1)
     seq = lane // LEN
@@ -258,6 +271,7 @@
     L[c, 0, b, a, 4] = jnp.where(place == 3, ids_ref[y], piece)
     mine_block = L.at[c, 0, b, a, 4]
 
+    pl.semaphore_wait(inside.at[1], 2)
     zs = {}
     for k in (8, 9, 7, 10, 6, 11, 5, 12, 4, 13, 3, 14, 2, 15, 1):
         rel = (4 - k) % NZ
@@ -524,6 +538,7 @@
             pltpu.VMEM((SLOTS, NEGS), jnp.int32),
             pltpu.VMEM((SLOTS, NEGS), jnp.int32),
             dma((10,)),
+            pltpu.SemaphoreType.REGULAR((2,)),
             pltpu.VMEM((1, TOK), f32),
             pltpu.VMEM((NT, 1, TOK), f32),
             pltpu.VMEM((1, TOK), f32),

time: 68 us -> 66.1 us (0.972)
  Pallas kernels: 67.2 us -> 65.3 us
    pallas_call x1, Pallas kernels: 63.9 us -> 62 us  [body(): pl.pallas_call(run, out_shape=(jax.ShapeDtypeStruct((16, F), f32), jax.Sh...]
where the time goes in v4:
time: 66.1 us; the launch traced here: 65.9 us
  Pallas kernels  65.3 us (99%)
    pallas_call x1, Pallas kernels, body(): pl.pallas_call(run, out_shape=(jax.ShapeDtypeStruct((16, F), f32), jax.Sh...  62 us
    pallas_call x1, Pallas kernels, body(): pl.pallas_call(finish_kernel, out_shape=(state_out,) * 3 + tuple((jax.Sha...  3.25 us

profile of v4, /device:TPU:1, one launch (start us, length us, event | category | flops | bytes accessed | tf_op | source)
XLA Modules:
  0.0 65.9 jit_solution(7793002879347340167)
XLA Ops:
  0.6 62.0 %shard_map.145 = (f32[16,512]{1,0:T(8,128)}, f32[8,768]{1,0:T(8,128)}, bf16[512,768]{1,0:T(8,128)(2,1)}, f32[1,512]{1,0:T(1,128)}, f32[1,1]{1,0:T(1,128)}) custom-call(bf16[256,512]{1,0:T(8,128)(2,1)} %bitcast.9, bf16[256,512]{1,0:T(8,128)(2,1)} %bitcast.11, bf16[256,512]{1,0:T(8,128)(2,1)} %bitcast.13, s32[4]{0:T(128)} %l0.1, s32[4]{0:T(128)} %l1.1, s32[4]{0:T(128)} %l2.1, ...), custom_call_target="tpu_custom_call" | custom-call | tf_op jit(solution)/shard_map/pallas_call | solution.py:516
  62.7 3.3 %shard_map.146 = (bf16[256,512]{1,0:T(8,128)(2,1)}, bf16[256,512]{1,0:T(8,128)(2,1)}, bf16[256,512]{1,0:T(8,128)(2,1)}, bf16[512,768]{1,0:T(8,128)(2,1)}, f32[1,512]{1,0:T(1,128)}, /*index=5*/f32[1,1]{1,0:T(1,128)}) custom-call(bf16[256,512]{1,0:T(8,128)(2,1)} %bitcast.10, bf16[256,512]{1,0:T(8,128)(2,1)} %bitcast.12, bf16[256,512]{1,0:T(8,128)(2,1)} %bitcast.14, ...), custom_call_target="tpu_custom_call" | custom-call | tf_op jit(solution)/shard_map/pallas_call | solution.py:579

commit v5 on v4

--- a/solution.py
+++ b/solution.py
@@ -404,7 +404,15 @@
     d_up = dot3(split2(g_in.T), uq)
     d_un = dot3(split2(g_neg.T), uq)
     d_unit = jnp.concatenate([d_uq, d_up, d_un], 0)
-    dproj[...] = (d_unit - unit * jnp.sum(unit * d_unit, -1, keepdims=True)) * r_norm
+    at_in = g_in * s_in
+    at_neg = g_neg * s_neg
+    columns = jnp.concatenate(
+        [jnp.sum(at_in, 0, keepdims=True), jnp.sum(at_neg, 0, keepdims=True), jnp.zeros((6, ALL), f32)], 0
+    ).T
+    along = jnp.concatenate(
+        [jnp.sum(at_in + at_neg, 1, keepdims=True), columns[:, 0:1], columns[:, 1:2]], 0
+    ) / score_scale
+    dproj[...] = (d_unit - unit * along) * r_norm
 
     px_relay(1, px1)
 
@@ -437,14 +445,14 @@
             ],
             0,
         )
-        parts[i] = dot3(split2(plains), split2(projs), TN)
-
-    for k in (0, 1, 3):
-        line_part((x + k) % NX)
+        return dot3(split2(plains), split2(projs), TN)
+
+    parts[0] = line_part(x)
+    parts[1] = line_part((x + 1) % NX)
+    parts[1] = parts[1] + line_part((x + 3) % NX)
     for cp in px0[2:] + px1[2:]:
         cp.wait()
-    line_part((x + 2) % NX)
-    grad = ((parts[0] + parts[1]) + (parts[2] + parts[3])) / loss_scale
+    grad = ((parts[0] + line_part((x + 2) % NX)) + parts[1]) / loss_scale
     weighted = grad * w_ref[...].astype(f32)
     fold = weighted[:, 0:128]
     for i in range(1, E // 128):
@@ -551,7 +559,7 @@
             pltpu.VMEM((SEQ, E), bf16),
             pltpu.VMEM((SEQ, E), bf16),
             pltpu.VMEM((SEQ, E), f32),
-            pltpu.VMEM((NX, F, E), f32),
+            pltpu.VMEM((2, F, E), f32),
             pltpu.VMEM((16, E), f32),
             dma((NT - 1,)),
             dma((NT - 1,)),

time: 66.1 us -> 64.3 us (0.973)
  Pallas kernels: 65.3 us -> 63.5 us
    pallas_call x1, Pallas kernels: 62 us -> 60.2 us  [body(): pl.pallas_call(run, out_shape=(jax.ShapeDtypeStruct((16, F), f32), jax.Sh...]
where the time goes in v5:
time: 64.3 us; the launch traced here: 64.1 us
  Pallas kernels  63.5 us (99%)
    pallas_call x1, Pallas kernels, body(): pl.pallas_call(run, out_shape=(jax.ShapeDtypeStruct((16, F), f32), jax.Sh...  60.2 us
    pallas_call x1, Pallas kernels, body(): pl.pallas_call(finish_kernel, out_shape=(state_out,) * 3 + tuple((jax.Sha...  3.25 us

profile of v5, /device:TPU:1, one launch (start us, length us, event | category | flops | bytes accessed | tf_op | source)
XLA Modules:
  0.0 64.1 jit_solution(501525718866876708)
XLA Ops:
  0.6 60.2 %shard_map.145 = (f32[16,512]{1,0:T(8,128)}, f32[8,768]{1,0:T(8,128)}, bf16[512,768]{1,0:T(8,128)(2,1)}, f32[1,512]{1,0:T(1,128)}, f32[1,1]{1,0:T(1,128)}) custom-call(bf16[256,512]{1,0:T(8,128)(2,1)} %bitcast.9, bf16[256,512]{1,0:T(8,128)(2,1)} %bitcast.11, bf16[256,512]{1,0:T(8,128)(2,1)} %bitcast.13, s32[4]{0:T(128)} %l0.1, s32[4]{0:T(128)} %l1.1, s32[4]{0:T(128)} %l2.1, ...), custom_call_target="tpu_custom_call" | custom-call | tf_op jit(solution)/shard_map/pallas_call | solution.py:524
  60.8 3.3 %shard_map.146 = (bf16[256,512]{1,0:T(8,128)(2,1)}, bf16[256,512]{1,0:T(8,128)(2,1)}, bf16[256,512]{1,0:T(8,128)(2,1)}, bf16[512,768]{1,0:T(8,128)(2,1)}, f32[1,512]{1,0:T(1,128)}, /*index=5*/f32[1,1]{1,0:T(1,128)}) custom-call(bf16[256,512]{1,0:T(8,128)(2,1)} %bitcast.10, bf16[256,512]{1,0:T(8,128)(2,1)} %bitcast.12, bf16[256,512]{1,0:T(8,128)(2,1)} %bitcast.14, ...), custom_call_target="tpu_custom_call" | custom-call | tf_op jit(solution)/shard_map/pallas_call | solution.py:587
